TPU v7x, 32 devices: a whole 2x2x4 slice. The times are simulated.
32 devices in a mesh: samples: 2 (over y), grid: 16 (over z, x, core).
Axes of the slice: x: 2, y: 2, z: 4, core: 2. Of those that a mesh axis runs over, the one named last changes fastest.
Arguments:
- hamiltonian: float32 [64, 4, 128, 128], P('grid'), may hold values from -0.25 to 0.25
- columns: int32 [64, 4], P('grid'), may hold values from 0 to 63, as said below
- sample: int32 [2], P('samples'), parts along dimension 0, may hold values from 0 to 1023
Outputs:
- density: float32 [128, 4, 128, 128], P(('samples', 'grid')), parts along dimension 0
There are 2 independent parts, one for each index of `samples`. A program takes and returns all parts, laid end to end along the dimension named above; an argument that names none is the same for every part. Nothing has to cross between parts.
Inputs may be any that keep to these rules, and one draw needn't show every extreme that they name: `columns`: each row's entries are distinct and sorted, lie within cyclic distance 3 of the row's own index (modulo 64), and include the row's own index.
All inputs are finite; a program needn't handle non-finite values.
Results may differ from a plain program's by a relative error of at most 0.0003.
Values sent between devices are 32-bit elements; how exact they have to be, the bound alone decides.
A program may use at most 64 MiB of HBM per device.

v0:
```python
import jax
import jax.numpy as jnp
from jax import lax
from jax.sharding import PartitionSpec as P

REACH = 3
STEPS = 2


def shifted(value, axis, steps):
    count = lax.axis_size(axis)
    pairs = [(source, (source + steps) % count) for source in range(count)]
    return lax.ppermute(value, axis, pairs)


def padded(shard, sides, width):
    for axis, dim in sides:
        peers, length = (lax.axis_size(axis), shard.shape[dim])
        up = [(i, (i + 1) % peers) for i in range(peers)]
        down = [(j, i) for i, j in up]
        last = lax.slice_in_dim(shard, length - width, length, axis=dim)
        leading = lax.slice_in_dim(shard, 0, width, axis=dim)
        before = lax.ppermute(last, axis, up)
        after = lax.ppermute(leading, axis, down)
        shard = jnp.concatenate([before, shard, after], axis=dim)
    return shard


def radical_of(sample):
    places = jnp.arange(10, dtype=jnp.int32)
    sample_bits = jnp.bitwise_and(jnp.right_shift(sample[0], places), 1).astype(jnp.float32)
    return jnp.sum(sample_bits * jnp.power(jnp.float32(0.5), (places + 1).astype(jnp.float32)))


def extend_tiles(tiles, window):
    below = shifted(tiles, "grid", 1)
    above = shifted(tiles, "grid", -1)
    return jnp.concatenate([below[below.shape[0] - window :], tiles, above[:window]], axis=0)


def shards(hamiltonian, columns, sample):
    devices = lax.axis_size("grid")
    position = lax.axis_index("grid")
    window = REACH
    local_rows = hamiltonian.shape[0]
    total_rows = devices * local_rows
    first_row = position * local_rows
    chemical = -0.2 + 0.4 * radical_of(sample)
    row_ids = (first_row + jnp.arange(local_rows, dtype=jnp.int32))[:, None]
    ondiag = (columns == row_ids).astype(jnp.float32)[:, :, None, None]
    identity = jnp.eye(hamiltonian.shape[-1], dtype=jnp.float32)
    density = 0.4 * (chemical * ondiag * identity - hamiltonian) + 0.5 * ondiag * identity
    extended_columns = padded(columns, (("grid", 0),), window)
    offsets = jnp.mod(columns - first_row + window, total_rows)
    remote_columns = jnp.take(extended_columns, offsets, axis=0)
    matches = (remote_columns[:, :, :, None] == columns[:, None, None, :]).astype(jnp.float32)
    for iteration in range(STEPS):
        extended_tiles = extend_tiles(density, window)
        gathered = jnp.take(extended_tiles, offsets, axis=0)
        products = jnp.einsum(
            "raxy,ramyz->ramxz", density, gathered, precision=lax.Precision.HIGHEST
        )
        square = jnp.einsum("ramb,ramxz->rbxz", matches, products, precision=lax.Precision.HIGHEST)
        products = jnp.einsum(
            "raxy,ramyz->ramxz", square, gathered, precision=lax.Precision.HIGHEST
        )
        cube = jnp.einsum("ramb,ramxz->rbxz", matches, products, precision=lax.Precision.HIGHEST)
        density = 3.0 * square - 2.0 * cube
    return density


def solution(mesh):
    return jax.shard_map(
        shards,
        mesh=mesh,
        in_specs=(P("grid", None, None, None), P("grid", None), P("samples")),
        out_specs=P(("samples", "grid"), None, None, None),
        check_vma=False,
    )
```

profile of v0, /device:TPU:1, one launch (start us, length us, event | category | flops | bytes accessed | tf_op | source)
XLA Modules:
  0.0 148.2 jit_solution(9762557544578424114)
XLA Ops:
  2.6 1.5 %multiply_add_fusion = f32[4,4,128,128]{3,2,1,0:T(8,128)S(1)} fusion(f32[4,4,128,128]{3,2,1,0:T(8,128)} %param.5, f32[4,4]{1,0:T(4,128)S(1)} %broadcast_select_fusion.1, f32[128,128]{1,0:T(8,128)S(1)} %fusion.36, f32[4,4]{1,0:T(4,128)S(1)} %get-tuple-element.8), kind=kLoop, calls=%fused_computation.37 | loop fusion | flops 1310720 | bytes 2162816 | tf_op jit(solution)/shard_map/add | solution.py:52
  4.1 2.7 %collective-permute-start.2 = (f32[4,4,128,128]{3,2,1,0:T(8,128)S(1)}, f32[4,4,128,128]{3,2,1,0:T(8,128)S(1)}, u32[]{:S(2)}, u32[]{:S(2)}) collective-permute-start(f32[4,4,128,128]{3,2,1,0:T(8,128)S(1)} %multiply_add_fusion), channel_id=1, source_target_pairs={{0,1},{1,2},{2,3},{3,4},{4,5},{5,6},{6,7},{7,8},{8,9},{9,10},{10,1... | collective-permute-start | bytes 3145736 | tf_op jit(solution)/shard_map/ppermute | solution.py:13
  7.5 1.7 %collective-permute-start = (s32[3,4]{1,0:T(4,128)S(1)}, s32[3,4]{1,0:T(4,128)S(1)}, u32[]{:S(2)}, u32[]{:S(2)}) collective-permute-start(s32[3,4]{1,0:T(4,128)S(1)} %get-tuple-element.10), channel_id=1, source_target_pairs={{0,1},{1,2},{2,3},{3,4},{4,5},{5,6},{6,7},{7,8},{8,9},{9,10},{10,1... | collective-permute-start | bytes 152 | tf_op jit(solution)/shard_map/ppermute | solution.py:23
  9.3 1.2 collective-permute-start.1
  11.3 18.5 %collective-permute-done = s32[3,4]{1,0:T(4,128)S(1)} collective-permute-done((s32[3,4]{1,0:T(4,128)S(1)}, s32[3,4]{1,0:T(4,128)S(1)}, u32[]{:S(2)}, u32[]{:S(2)}) %collective-permute-start) | collective-permute-done | bytes 80 | tf_op jit(solution)/shard_map/ppermute | solution.py:23
  29.8 2.5 %collective-permute-done.1 = s32[3,4]{1,0:T(4,128)S(1)} collective-permute-done((s32[3,4]{1,0:T(4,128)S(1)}, s32[3,4]{1,0:T(4,128)S(1)}, u32[]{:S(2)}, u32[]{:S(2)}) %collective-permute-start.1) | collective-permute-done | bytes 80 | tf_op jit(solution)/shard_map/ppermute | solution.py:24
  33.9 1.4 pad_maximum_fusion
  35.3 2.8 %gather_fusion.1 = f32[16,4,128,128]{3,2,1,0:T(8,128)} fusion(f32[10,4,128,128]{3,2,1,0:T(8,128)S(1)} %pad_maximum_fusion, s32[1024]{0:T(1024)S(1)} %pad_clamp_fusion), kind=kCustom, calls=%fused_computation.clone | custom fusion | bytes 8388672 | tf_op jit(solution)/shard_map/jit(_take)/gather | solution.py:59
  38.1 5.3 %copy.16 = f32[4,4,4,128,128]{3,4,2,1,0:T(8,128)} copy(f32[4,4,4,128,128]{4,3,2,1,0:T(8,128)} %bitcast.63) | data formatting | bytes 8388608 | tf_op jit(solution)/shard_map/jit(_take)/gather | solution.py:59
  43.5 7.0 %fusion.8 = f32[4,4,4,128,128]{3,4,2,1,0:T(8,128)} fusion(f32[4,4,4,128,128]{3,4,2,1,0:T(8,128)} %copy.16, pred[4,4]{1,0:T(4,128)(4,1)S(1)} %get-tuple-element.6, f32[4,4,128,128]{3,2,1,0:T(8,128)S(1)} %copy-done.3), kind=kOutput, calls=%fused_computation.13 | convolution fusion | flops 1611661312 | bytes 9437200 | tf_op jit(solution)/shard_map/raxy,ramyz->ramxz/dot_general | solution.py:60
  50.4 5.5 %copy.17 = f32[4,4,4,128,128]{4,2,1,3,0:T(4,128)} copy(f32[4,4,4,128,128]{3,4,2,1,0:T(8,128)} %fusion.8) | data formatting | bytes 8388608 | tf_op jit(solution)/shard_map/raxy,ramyz->ramxz/transpose | solution.py:60
  55.9 5.8 %fusion.41 = f32[4,4,128,128,1]{3,1,4,2,0:T(4,128)S(1)} fusion(f32[4,4,4,128,128]{4,2,1,3,0:T(4,128)} %copy.17, s32[4,4]{1,0:T(4,128)S(1)} %copy-done.6, s32[4,4,4]{2,1,0:T(4,128)S(1)} %copy.15), kind=kOutput, calls=%fused_computation.44 | convolution fusion | flops 50331904 | bytes 5243200 | tf_op jit(solution)/shard_map/ramb,ramxz->rbxz/dot_general | solution.py:63
  61.7 5.4 %fusion.11 = f32[4,4,4,128,128]{3,4,2,1,0:T(8,128)} fusion(f32[4,4,4,128,128]{3,4,2,1,0:T(8,128)S(1)} %copy-done.1, pred[4,4]{1,0:T(4,128)(4,1)S(1)} %get-tuple-element.6, f32[4,4,128,128,1]{3,1,2,0,4:T(4,128)S(1)} %bitcast.66), kind=kOutput, calls=%fused_computation.14 | convolution fusion | flops 1611661312 | bytes 9437200 | tf_op jit(solution)/shard_map/raxy,ramyz->ramxz/dot_general | solution.py:64
  67.1 5.5 %copy.19 = f32[4,4,4,128,128]{4,2,1,3,0:T(4,128)} copy(f32[4,4,4,128,128]{3,4,2,1,0:T(8,128)} %fusion.11) | data formatting | bytes 8388608 | tf_op jit(solution)/shard_map/raxy,ramyz->ramxz/transpose | solution.py:64
  72.6 5.8 %fusion.30 = f32[4,4,128,128]{3,1,2,0:T(4,128)S(1)} fusion(f32[4,4,4,128,128]{4,2,1,3,0:T(4,128)} %copy.19, f32[4,4,128,128,1]{3,1,4,2,0:T(4,128)S(1)} %fusion.41, s32[4,4]{1,0:T(4,128)S(1)} %copy-done.6, s32[4,4,4]{2,1,0:T(4,128)S(1)} %copy.15), kind=kOutput, calls=%fused_computation.29 | convolution fusion | flops 51118336 | bytes 6291776 | tf_op jit(solution)/shard_map/ramb,ramxz->rbxz/dot_general | solution.py:67
  78.9 22.5 %collective-permute-done.4 = f32[4,4,128,128]{3,1,2,0:T(4,128)S(1)} collective-permute-done((f32[4,4,128,128]{3,1,2,0:T(4,128)S(1)}, f32[4,4,128,128]{3,1,2,0:T(4,128)S(1)}, u32[]{:S(2)}, u32[]{:S(2)}) %collective-permute-start.4) | collective-permute-done | bytes 1048608 | tf_op jit(solution)/shard_map/ppermute | solution.py:13
  102.2 4.8 %gather_fusion.2 = f32[16,4,128,128]{3,1,2,0:T(4,128)} fusion(f32[10,4,128,128]{3,1,2,0:T(4,128)S(1)} %pad_maximum_fusion.1, s32[1024]{0:T(1024)S(1)} %pad_clamp_fusion), kind=kCustom, calls=%fused_computation.1.clone | custom fusion | bytes 8388672 | tf_op jit(solution)/shard_map/jit(_take)/gather | solution.py:59
  106.9 5.3 %copy.20 = f32[4,4,4,128,128]{3,4,2,1,0:T(8,128)} copy(f32[4,4,4,128,128]{4,2,3,1,0:T(4,128)} %bitcast.62) | data formatting | bytes 8388608 | tf_op jit(solution)/shard_map/jit(_take)/gather | solution.py:59
  112.3 7.0 %fusion.14 = f32[4,4,4,128,128]{3,4,2,1,0:T(8,128)} fusion(f32[4,4,4,128,128]{3,4,2,1,0:T(8,128)} %copy.20, pred[4,4]{1,0:T(4,128)(4,1)S(1)} %get-tuple-element.6, f32[4,4,128,128,1]{3,1,2,0,4:T(4,128)S(1)} %bitcast.64), kind=kOutput, calls=%fused_computation.15 | convolution fusion | flops 1611661312 | bytes 9437200 | tf_op jit(solution)/shard_map/raxy,ramyz->ramxz/dot_general | solution.py:60
  119.2 5.5 %copy.22 = f32[4,4,4,128,128]{4,2,1,3,0:T(4,128)} copy(f32[4,4,4,128,128]{3,4,2,1,0:T(8,128)} %fusion.14) | data formatting | bytes 8388608 | tf_op jit(solution)/shard_map/raxy,ramyz->ramxz/transpose | solution.py:60
  124.7 5.8 %fusion.38 = f32[4,4,128,128,1]{3,1,4,2,0:T(4,128)S(1)} fusion(f32[4,4,4,128,128]{4,2,1,3,0:T(4,128)} %copy.22, s32[4,4]{1,0:T(4,128)S(1)} %copy-done.6, s32[4,4,4]{2,1,0:T(4,128)S(1)} %copy.15), kind=kOutput, calls=%fused_computation.41 | convolution fusion | flops 50331904 | bytes 5243200 | tf_op jit(solution)/shard_map/ramb,ramxz->rbxz/dot_general | solution.py:63
  130.5 5.4 %fusion.17 = f32[4,4,4,128,128]{3,4,2,1,0:T(8,128)} fusion(f32[4,4,4,128,128]{3,4,2,1,0:T(8,128)S(1)} %copy-done, pred[4,4]{1,0:T(4,128)(4,1)S(1)} %get-tuple-element.6, f32[4,4,128,128,1]{3,1,2,0,4:T(4,128)S(1)} %bitcast.65), kind=kOutput, calls=%fused_computation.16 | convolution fusion | flops 1611661312 | bytes 9437200 | tf_op jit(solution)/shard_map/raxy,ramyz->ramxz/dot_general | solution.py:64
  135.9 5.5 %copy.24 = f32[4,4,4,128,128]{4,2,1,3,0:T(4,128)} copy(f32[4,4,4,128,128]{3,4,2,1,0:T(8,128)} %fusion.17) | data formatting | bytes 8388608 | tf_op jit(solution)/shard_map/raxy,ramyz->ramxz/transpose | solution.py:64
  141.4 5.8 %fusion.31 = f32[4,4,128,128]{3,1,2,0:T(4,128)S(1)} fusion(f32[4,4,4,128,128]{4,2,1,3,0:T(4,128)} %copy.24, f32[4,4,128,128,1]{3,1,4,2,0:T(4,128)S(1)} %fusion.38, s32[4,4]{1,0:T(4,128)S(1)} %copy-done.6, s32[4,4,4]{2,1,0:T(4,128)S(1)} %copy.15), kind=kOutput, calls=%fused_computation.30 | convolution fusion | flops 51118336 | bytes 6291776 | tf_op jit(solution)/shard_map/ramb,ramxz->rbxz/dot_general | solution.py:67
  (40 shorter events, 7.0 us)
Async XLA Ops:
  4.1 29.7 %copy-start.2 = (f32[4,4,128,128]{3,2,1,0:T(8,128)}, f32[4,4,128,128]{3,2,1,0:T(8,128)S(1)}, u32[]{:S(2)}) copy-start(f32[4,4,128,128]{3,2,1,0:T(8,128)S(1)} %multiply_add_fusion) | copy-start | bytes 3145732
  4.1 29.6 %collective-permute-start.2 = (f32[4,4,128,128]{3,2,1,0:T(8,128)S(1)}, f32[4,4,128,128]{3,2,1,0:T(8,128)S(1)}, u32[]{:S(2)}, u32[]{:S(2)}) collective-permute-start(f32[4,4,128,128]{3,2,1,0:T(8,128)S(1)} %multiply_add_fusion), channel_id=1, source_target_pairs={{0,1},{1,2},{2,3},{3,4},{4,5},{5,6},{6,7},{7,8},{8,9},{9,10},{10,1... | collective-permute-start | bytes 3145736 | tf_op jit(solution)/shard_map/ppermute | solution.py:13
  6.8 27.1 %collective-permute-start.3 = (f32[4,4,128,128]{3,2,1,0:T(8,128)S(1)}, f32[4,4,128,128]{3,2,1,0:T(8,128)S(1)}, u32[]{:S(2)}, u32[]{:S(2)}) collective-permute-start(f32[4,4,128,128]{3,2,1,0:T(8,128)S(1)} %multiply_add_fusion), channel_id=1, source_target_pairs={{0,15},{1,0},{2,1},{3,2},{4,3},{5,4},{6,5},{7,6},{8,7},{9,8},{10,9... | collective-permute-start | bytes 3145736 | tf_op jit(solution)/shard_map/ppermute | solution.py:13
  7.5 22.3 %collective-permute-start = (s32[3,4]{1,0:T(4,128)S(1)}, s32[3,4]{1,0:T(4,128)S(1)}, u32[]{:S(2)}, u32[]{:S(2)}) collective-permute-start(s32[3,4]{1,0:T(4,128)S(1)} %get-tuple-element.10), channel_id=1, source_target_pairs={{0,1},{1,2},{2,3},{3,4},{4,5},{5,6},{6,7},{7,8},{8,9},{9,10},{10,1... | collective-permute-start | bytes 152 | tf_op jit(solution)/shard_map/ppermute | solution.py:23
  9.3 23.0 %collective-permute-start.1 = (s32[3,4]{1,0:T(4,128)S(1)}, s32[3,4]{1,0:T(4,128)S(1)}, u32[]{:S(2)}, u32[]{:S(2)}) collective-permute-start(s32[3,4]{1,0:T(4,128)S(1)} %get-tuple-element.11), channel_id=1, source_target_pairs={{1,0},{2,1},{3,2},{4,3},{5,4},{6,5},{7,6},{8,7},{9,8},{10,9},{11,1... | collective-permute-start | bytes 152 | tf_op jit(solution)/shard_map/ppermute | solution.py:24
  38.1 5.3 %copy-start.3 = (f32[4,4,128,128]{3,2,1,0:T(8,128)S(1)}, f32[4,4,128,128]{3,2,1,0:T(8,128)}, u32[]{:S(2)}) copy-start(f32[4,4,128,128]{3,2,1,0:T(8,128)} %copy-done.2) | copy-start | bytes 3145732
  50.4 5.5 %copy-start.6 = (s32[4,4]{1,0:T(4,128)S(1)}, s32[4,4]{1,0:T(4,128)}, u32[]{:S(2)}) copy-start(s32[4,4]{1,0:T(4,128)} %param.6) | copy-start | bytes 196
  55.9 5.8 %copy-start.1 = (f32[4,4,4,128,128]{3,4,2,1,0:T(8,128)S(1)}, f32[4,4,4,128,128]{3,4,2,1,0:T(8,128)}, u32[]{:S(2)}) copy-start(f32[4,4,4,128,128]{3,4,2,1,0:T(8,128)} %copy.16) | copy-start | bytes 12582916
  78.3 23.2 %copy-start.4 = (f32[4,4,128,128]{3,1,2,0:T(4,128)}, f32[4,4,128,128]{3,1,2,0:T(4,128)S(1)}, u32[]{:S(2)}) copy-start(f32[4,4,128,128]{3,1,2,0:T(4,128)S(1)} %fusion.30) | copy-start | bytes 3145732
  78.4 23.0 %collective-permute-start.4 = (f32[4,4,128,128]{3,1,2,0:T(4,128)S(1)}, f32[4,4,128,128]{3,1,2,0:T(4,128)S(1)}, u32[]{:S(2)}, u32[]{:S(2)}) collective-permute-start(f32[4,4,128,128]{3,1,2,0:T(4,128)S(1)} %fusion.30), channel_id=1, source_target_pairs={{0,1},{1,2},{2,3},{3,4},{4,5},{5,6},{6,7},{7,8},{8,9},{9,10},{10,1... | collective-permute-start | bytes 3145736 | tf_op jit(solution)/shard_map/ppermute | solution.py:13
  78.4 23.0 %collective-permute-start.5 = (f32[4,4,128,128]{3,1,2,0:T(4,128)S(1)}, f32[4,4,128,128]{3,1,2,0:T(4,128)S(1)}, u32[]{:S(2)}, u32[]{:S(2)}) collective-permute-start(f32[4,4,128,128]{3,1,2,0:T(4,128)S(1)} %fusion.30), channel_id=1, source_target_pairs={{0,15},{1,0},{2,1},{3,2},{4,3},{5,4},{6,5},{7,6},{8,7},{9,8},{10,9... | collective-permute-start | bytes 3145736 | tf_op jit(solution)/shard_map/ppermute | solution.py:13
  106.9 5.3 %copy-start.5 = (f32[4,4,128,128]{3,1,2,0:T(4,128)S(1)}, f32[4,4,128,128]{3,1,2,0:T(4,128)}, u32[]{:S(2)}) copy-start(f32[4,4,128,128]{3,1,2,0:T(4,128)} %copy-done.4) | copy-start | bytes 3145732
  124.7 5.8 %copy-start = (f32[4,4,4,128,128]{3,4,2,1,0:T(8,128)S(1)}, f32[4,4,4,128,128]{3,4,2,1,0:T(8,128)}, u32[]{:S(2)}) copy-start(f32[4,4,4,128,128]{3,4,2,1,0:T(8,128)} %copy.20) | copy-start | bytes 12582916
where the time goes:
time: 149 us; the launch traced here: 148 us
  matrix products  47.8 us (32%)
  waiting for transfers between devices  43.5 us (29%)
  local copies, waits for them, and re-layouts  43.1 us (29%)
  other arithmetic  6.33 us (4%)
  starting transfers between devices  6.15 us (4%)
    dot_general x4, matrix products, shards(): jnp.einsum('ramb,ramxz->rbxz', matches, products, precision=lax.Precision...  23.1 us
    ppermute x4, waiting for transfers between devices, shifted(): return lax.ppermute(value, axis, pairs)  22.5 us
    ppermute x1, waiting for transfers between devices, padded(): before = lax.ppermute(last, axis, up)  18.5 us
    gather x4, local copies, waits for them, and re-layouts, shards(): gathered = jnp.take(extended_tiles, offsets, axis=0)  18.2 us
    dot_general x2, matrix products, shards(): jnp.einsum('raxy,ramyz->ramxz', density, gathered, precision=lax.Precisio...  13.9 us
    transpose x2, local copies, waits for them, and re-layouts, shards(): jnp.einsum('raxy,ramyz->ramxz', density, gathered, precision=lax.Precisio...  10.9 us
    transpose x2, local copies, waits for them, and re-layouts, shards(): jnp.einsum('raxy,ramyz->ramxz', square, gathered, precision=lax.Precision...  10.9 us
    dot_general x2, matrix products, shards(): jnp.einsum('raxy,ramyz->ramxz', square, gathered, precision=lax.Precision...  10.7 us
  transfers between devices with their start and end apart: 6, of which 3 were waited for; matrix products, arithmetic and copies ran while one was open for 2% of the time, Pallas kernels for 0%

commit v1 on v0

v1 whole, which is shorter than its diff:
```python
import functools

import jax
import jax.numpy as jnp
from jax import lax
from jax.experimental import pallas as pl
from jax.experimental.pallas import tpu as pltpu
from jax.sharding import PartitionSpec as P

REACH = 3
STEPS = 2
ROWS = 4
HALO = STEPS * REACH
SPAN = ROWS + 2 * HALO
MESH = pl.DeviceIdType.MESH

ORDER = ((5, 0), (6, 0), (7, 0), (8, 0), (4, 0), (9, 0), (3, 0), (6, 1), (10, 0), (7, 1), (11, 0), (8, 1), (12, 0), (9, 1))


def pick(index, values):
    chosen = jnp.int32(values[0])
    for at, value in enumerate(values[1:], 1):
        chosen = jnp.where(index == at, jnp.int32(value), chosen)
    return chosen


def kernel(
    devices, ham, columns, sample, out, ext, cbuf, csm, high, low, eye, ahigh, alow, left, left2,
    recv, send, crecv, csend, local, csem,
):
    me, s = lax.axis_index("grid"), lax.axis_index("samples")
    slots, tile = ham.shape[1], ham.shape[2]
    pair = slots // 2
    total = devices * ROWS
    zero_tile = SPAN * slots
    odd = lax.rem(me, 2)
    sign = 2 * odd - 1

    def at(offset):
        return (s, lax.rem(me + offset + devices, devices))

    mate, outer, behind, beyond = at(-sign), at(sign), at(-2 * sign), at(2 * sign)
    peer = (1 - s, me)

    def own(u):
        return jnp.where(odd == 1, u - HALO, HALO + ROWS - 1 - u)

    def mine(u):
        return ext.at[u, pl.ds(pair * s, pair)]

    def theirs(u):
        return ext.at[u, pl.ds(pair * (1 - s), pair)]

    def copy(source, target, send_sem, recv_sem, device):
        return pltpu.make_async_remote_copy(
            src_ref=source, dst_ref=target, send_sem=send_sem, recv_sem=recv_sem, device_id=device, device_id_type=MESH
        )

    def to_mate(u):
        return copy(ham.at[own(u)], ext.at[11 - u], send.at[u - 6], recv.at[11 - u, 0], mate)

    def to_outer(u):
        return copy(ham.at[own(u), pl.ds(pair * s, pair)], mine(19 - u), send.at[4 + u - 6], recv.at[19 - u, s], outer)

    def to_behind(u):
        return copy(ham.at[own(u), pl.ds(pair * s, pair)], mine(u + 8), send.at[8 + u - 6], recv.at[u + 8, s], behind)

    def mine_to_peer(u):
        return copy(mine(u), mine(u), send.at[10 + u - 10], recv.at[u, s], peer)

    def mine_to_mate(u):
        return copy(mine(u), mine(11 - u), send.at[16 + u - 10], recv.at[11 - u, s], mate)

    def theirs_to_mate(u):
        return copy(theirs(u), theirs(11 - u), send.at[18 + u - 10], recv.at[11 - u, 1 - s], mate)

    def theirs_from_peer(u):
        return copy(theirs(u), theirs(u), send.at[10 + u - 10], recv.at[u, 1 - s], peer)

    def keep(u):
        return pltpu.make_async_copy(ham.at[own(u)], ext.at[u], local.at[u - 6])

    def columns_to(index):
        slot, device = ((1, mate), (3, outer), (4, behind), (0, beyond))[index]
        return copy(cbuf.at[2], cbuf.at[slot], csend.at[index], crecv.at[slot], device)

    barrier = pltpu.get_barrier_semaphore()
    for device in (mate, outer, behind, beyond, peer):
        pl.semaphore_signal(barrier, inc=1, device_id=device, device_id_type=MESH)
    for u in range(6, 10):
        keep(u).start()
    cbuf[2, 0:ROWS, 0:slots] = columns[...]
    pl.semaphore_wait(barrier, 5)

    for index in range(4):
        columns_to(index).start()
    for u in (9, 8, 7, 6):
        to_outer(u).start()
    for u in (6, 7):
        to_behind(u).start()
    for u in (6, 7, 8, 9):
        to_mate(u).start()

    same = lax.broadcasted_iota(jnp.int32, (tile, tile), 0) == lax.broadcasted_iota(jnp.int32, (tile, tile), 1)
    eye[...] = same.astype(jnp.float32)
    for step in range(STEPS):
        high[step, zero_tile] = jnp.zeros((tile, tile), jnp.bfloat16)
        low[step, zero_tile] = jnp.zeros((tile, tile), jnp.bfloat16)
    radical = jnp.float32(0.0)
    for bit in range(10):
        radical += (lax.shift_right_logical(sample[0], bit) & 1).astype(jnp.float32) * jnp.float32(0.5 ** (bit + 1))
    chemical = -0.2 + 0.4 * radical

    for index in range(4):
        columns_to(index).wait()
    table = pltpu.make_async_copy(cbuf, csm, csem)
    table.start()
    table.wait()

    def column(u, slot):
        place = (u + 2) & 3
        return csm[lax.shift_right_logical(u + 2, 2), jnp.where(odd == 1, place, 3 - place), slot]

    def row_of(col):
        up = jnp.clip(lax.rem(col - ROWS * me + HALO + total, total), 0, SPAN - 1)
        return jnp.where(odd == 1, up, SPAN - 1 - up)

    def split(value):
        upper = value.astype(jnp.bfloat16)
        return upper, (value - upper.astype(jnp.float32)).astype(jnp.bfloat16)

    def begin(u):
        for m in range(slots):
            diagonal = eye[...] * jnp.where(row_of(column(u, m)) == u, 1.0, 0.0)
            tiles = 0.4 * (chemical * diagonal - ext[u, m]) + 0.5 * diagonal
            upper, lower = split(tiles)
            high[0, u * slots + m] = upper
            low[0, u * slots + m] = lower

    def begin_each(first, last):
        def body(u, carry):
            begin(u)
            return carry

        lax.fori_loop(first, last, body, 0)

    def got(u):
        mine_to_peer(u).wait_recv()
        mine_to_peer(u).start()
        if u < 12:
            mine_to_mate(u).start()

    def got_rest(u):
        theirs_from_peer(u).wait_recv()
        if u < 12:
            theirs_to_mate(u).start()
        begin(u)

    def from_mate(u):
        mine_to_mate(11 - u).wait_recv()
        theirs_to_mate(11 - u).wait_recv()
        begin(u)

    def times(lefts):
        both = jnp.dot(lefts[...], ahigh[...], preferred_element_type=jnp.float32)
        rest = jnp.dot(lefts[0:tile], alow[...], preferred_element_type=jnp.float32)
        return both[0:tile] + (both[tile:] + rest)

    def work(u, step):
        own_columns = [column(u, b) for b in range(slots)]
        for a in range(slots):
            row = row_of(own_columns[a])
            held = [column(row, m) for m in range(slots)]
            for b in range(slots):
                index = jnp.int32(zero_tile)
                for m in range(slots):
                    index = jnp.where(held[m] == own_columns[b], row * slots + m, index)
                ahigh[a * tile : (a + 1) * tile, b * tile : (b + 1) * tile] = high[step, index]
                alow[a * tile : (a + 1) * tile, b * tile : (b + 1) * tile] = low[step, index]
        for m in range(slots):
            left[0:tile, m * tile : (m + 1) * tile] = high[step, u * slots + m]
            left[tile:, m * tile : (m + 1) * tile] = low[step, u * slots + m]
        square = times(left)
        upper, lower = split(square)
        left2[0:tile] = upper
        left2[tile:] = lower
        density = 3.0 * square - 2.0 * times(left2)

        @pl.when(step == 0)
        def _():
            upper, lower = split(density)
            for b in range(slots):
                high[1, u * slots + b] = upper[:, b * tile : (b + 1) * tile]
                low[1, u * slots + b] = lower[:, b * tile : (b + 1) * tile]

        @pl.when(step == 1)
        def _():
            for b in range(slots):
                out[own(u), b] = density[:, b * tile : (b + 1) * tile]

    for u in range(6, 10):
        keep(u).wait()
    for u in range(6, 10):
        to_mate(u).wait_recv()
    begin_each(2, 10)

    events = {
        2: lambda: (got(10), got(11), got_rest(10)),
        3: lambda: (got(12), got_rest(11)),
        4: lambda: (got(13), from_mate(1)),
        5: lambda: (got_rest(12),),
        6: lambda: (got(14), from_mate(0)),
        8: lambda: (got_rest(13),),
        10: lambda: (got(15), got_rest(14)),
        12: lambda: (got_rest(15),),
    }

    def body(turn, carry):
        for when, event in events.items():
            pl.when(turn == when)(lambda event=event: (event(), None)[1])
        work(pick(turn, [u for u, _ in ORDER]), pick(turn, [step for _, step in ORDER]))
        return carry

    lax.fori_loop(0, len(ORDER), body, 0)

    for u in (9, 8, 7, 6):
        to_outer(u).wait_send()
        to_mate(u).wait_send()
    for u in (6, 7):
        to_behind(u).wait_send()
    for u in range(10, 16):
        mine_to_peer(u).wait_send()
        if u < 12:
            mine_to_mate(u).wait_send()
            theirs_to_mate(u).wait_send()


def shards(hamiltonian, columns, sample):
    rows, slots, tile, _ = hamiltonian.shape
    devices = lax.axis_size("grid")
    assert rows == ROWS and devices >= 6
    dma = pltpu.SemaphoreType.DMA
    return pl.pallas_call(
        functools.partial(kernel, devices),
        out_shape=jax.ShapeDtypeStruct(hamiltonian.shape, jnp.float32),
        in_specs=[
            pl.BlockSpec(memory_space=pl.ANY),
            pl.BlockSpec(memory_space=pltpu.VMEM),
            pl.BlockSpec(memory_space=pltpu.SMEM),
        ],
        out_specs=pl.BlockSpec(memory_space=pltpu.VMEM),
        scratch_shapes=[
            pltpu.VMEM((SPAN, slots, tile, tile), jnp.float32),
            pltpu.VMEM((5, 8, 128), jnp.int32),
            pltpu.SMEM((5, 8, 128), jnp.int32),
            pltpu.VMEM((STEPS, SPAN * slots + 1, tile, tile), jnp.bfloat16),
            pltpu.VMEM((STEPS, SPAN * slots + 1, tile, tile), jnp.bfloat16),
            pltpu.VMEM((tile, tile), jnp.float32),
            pltpu.VMEM((slots * tile, slots * tile), jnp.bfloat16),
            pltpu.VMEM((slots * tile, slots * tile), jnp.bfloat16),
            pltpu.VMEM((2 * tile, slots * tile), jnp.bfloat16),
            pltpu.VMEM((2 * tile, slots * tile), jnp.bfloat16),
            dma((SPAN, 2)),
            dma((20,)),
            dma((5,)),
            dma((4,)),
            dma((4,)),
            dma,
        ],
        compiler_params=pltpu.CompilerParams(
            collective_id=0, has_side_effects=True, vmem_limit_bytes=40 * 2**20
        ),
    )(hamiltonian, columns, sample)


def solution(mesh):
    return jax.shard_map(
        shards,
        mesh=mesh,
        in_specs=(P("grid", None, None, None), P("grid", None), P("samples")),
        out_specs=P(("samples", "grid"), None, None, None),
        check_vma=False,
    )
```

time: 149 us -> 43 us (0.29)
  the two profiles are of different devices: /device:TPU:1 before, /device:TPU:16 now
where the time goes in v1:
time: 43 us; the launch traced here: 42.8 us
  Pallas kernels  39.3 us (91%)
  local copies, waits for them, and re-layouts  2.87 us (7%)
  between operations  0.67 us (2%)
    pallas_call x1, Pallas kernels, shards(): pl.pallas_call(functools.partial(kernel, devices), out_shape=jax.ShapeDty...  39.3 us
    unnamed x5, local copies, waits for them, and re-layouts  2.87 us

profile of v1, /device:TPU:16, one launch (start us, length us, event | category | flops | bytes accessed | tf_op | source)
XLA Modules:
  0.0 42.8 jit_solution(1614639517381446746)
XLA Ops:
  0.7 0.0 copy-start
  0.7 1.2 %copy-done = f32[4,4,128,128]{3,2,1,0:T(8,128)S(1)} copy-done((f32[4,4,128,128]{3,2,1,0:T(8,128)S(1)}, f32[4,4,128,128]{3,2,1,0:T(8,128)}, u32[]{:S(2)}) %copy-start) | copy-done | bytes 1048600
  1.9 0.0 copy-start.1
  1.9 0.7 %copy-done.1 = s32[4,4]{1,0:T(4,128)S(1)} copy-done((s32[4,4]{1,0:T(4,128)S(1)}, s32[4,4]{1,0:T(4,128)}, u32[]{:S(2)}) %copy-start.1) | copy-done | bytes 88
  2.6 39.3 %shard_map.37 = f32[4,4,128,128]{3,2,1,0:T(8,128)S(1)} custom-call(f32[4,4,128,128]{3,2,1,0:T(8,128)S(1)} %copy-done, s32[4,4]{1,0:T(4,128)S(1)} %copy-done.1, s32[1]{0:T(128)S(6)} %copy.5.sample), custom_call_target="tpu_custom_call" | custom-call | tf_op jit(solution)/shard_map/pallas_call | solution.py:243
  41.8 1.0 %copy.6 = f32[4,4,128,128]{3,2,1,0:T(8,128)} copy(f32[4,4,128,128]{3,2,1,0:T(8,128)S(1)} %shard_map.37) | data formatting | bytes 2097152
Async XLA Ops:
  0.7 1.2 %copy-start = (f32[4,4,128,128]{3,2,1,0:T(8,128)S(1)}, f32[4,4,128,128]{3,2,1,0:T(8,128)}, u32[]{:S(2)}) copy-start(f32[4,4,128,128]{3,2,1,0:T(8,128)} %ham.1) | copy-start | bytes 3145732
  1.9 0.7 %copy-start.1 = (s32[4,4]{1,0:T(4,128)S(1)}, s32[4,4]{1,0:T(4,128)}, u32[]{:S(2)}) copy-start(s32[4,4]{1,0:T(4,128)} %columns.1) | copy-start | bytes 196

commit v2 on v1

--- a/solution.py
+++ b/solution.py
@@ -14,7 +14,7 @@
 SPAN = ROWS + 2 * HALO
 MESH = pl.DeviceIdType.MESH
 
-ORDER = ((5, 0), (6, 0), (7, 0), (8, 0), (4, 0), (9, 0), (3, 0), (6, 1), (10, 0), (7, 1), (11, 0), (8, 1), (12, 0), (9, 1))
+ORDER = ((5, 0), (6, 0), (7, 0), (4, 0), (8, 0), (3, 0), (9, 0), (6, 1), (10, 0), (7, 1), (11, 0), (8, 1), (12, 0), (9, 1))
 
 
 def pick(index, values):
@@ -94,10 +94,8 @@
 
     for index in range(4):
         columns_to(index).start()
-    for u in (9, 8, 7, 6):
+    for u in (9, 8):
         to_outer(u).start()
-    for u in (6, 7):
-        to_behind(u).start()
     for u in (6, 7, 8, 9):
         to_mate(u).start()
 
@@ -149,6 +147,9 @@
         mine_to_peer(u).start()
         if u < 12:
             mine_to_mate(u).start()
+            to_outer(17 - u).start()
+        elif u < 14:
+            to_behind(u - 6).start()
 
     def got_rest(u):
         theirs_from_peer(u).wait_recv()
@@ -205,12 +206,13 @@
     begin_each(2, 10)
 
     events = {
-        2: lambda: (got(10), got(11), got_rest(10)),
-        3: lambda: (got(12), got_rest(11)),
-        4: lambda: (got(13), from_mate(1)),
-        5: lambda: (got_rest(12),),
-        6: lambda: (got(14), from_mate(0)),
-        8: lambda: (got_rest(13),),
+        0: lambda: (got(10),),
+        2: lambda: (got(11), got_rest(10)),
+        3: lambda: (from_mate(1),),
+        4: lambda: (got(12), got_rest(11)),
+        5: lambda: (from_mate(0),),
+        6: lambda: (got(13), got_rest(12)),
+        8: lambda: (got(14), got_rest(13)),
         10: lambda: (got(15), got_rest(14)),
         12: lambda: (got_rest(15),),
     }

time: 43 us -> 38.5 us (0.90)
  the two profiles are of different devices: /device:TPU:16 before, /device:TPU:0 now
where the time goes in v2:
time: 38.5 us; the launch traced here: 38.3 us
  Pallas kernels  34.8 us (90%)
  local copies, waits for them, and re-layouts  2.87 us (7%)
  between operations  0.67 us (2%)
    pallas_call x1, Pallas kernels, shards(): pl.pallas_call(functools.partial(kernel, devices), out_shape=jax.ShapeDty...  34.8 us
    unnamed x5, local copies, waits for them, and re-layouts  2.87 us

profile of v2, /device:TPU:0, one launch (start us, length us, event | category | flops | bytes accessed | tf_op | source)
XLA Modules:
  0.0 38.3 jit_solution(10493875342766395492)
XLA Ops:
  0.7 0.0 copy-start
  0.7 1.2 %copy-done = f32[4,4,128,128]{3,2,1,0:T(8,128)S(1)} copy-done((f32[4,4,128,128]{3,2,1,0:T(8,128)S(1)}, f32[4,4,128,128]{3,2,1,0:T(8,128)}, u32[]{:S(2)}) %copy-start) | copy-done | bytes 1048600
  1.9 0.0 copy-start.1
  1.9 0.7 %copy-done.1 = s32[4,4]{1,0:T(4,128)S(1)} copy-done((s32[4,4]{1,0:T(4,128)S(1)}, s32[4,4]{1,0:T(4,128)}, u32[]{:S(2)}) %copy-start.1) | copy-done | bytes 88
  2.6 34.8 %shard_map.37 = f32[4,4,128,128]{3,2,1,0:T(8,128)S(1)} custom-call(f32[4,4,128,128]{3,2,1,0:T(8,128)S(1)} %copy-done, s32[4,4]{1,0:T(4,128)S(1)} %copy-done.1, s32[1]{0:T(128)S(6)} %copy.5.sample), custom_call_target="tpu_custom_call" | custom-call | tf_op jit(solution)/shard_map/pallas_call | solution.py:245
  37.3 1.0 %copy.6 = f32[4,4,128,128]{3,2,1,0:T(8,128)} copy(f32[4,4,128,128]{3,2,1,0:T(8,128)S(1)} %shard_map.37) | data formatting | bytes 2097152
Async XLA Ops:
  0.7 1.2 %copy-start = (f32[4,4,128,128]{3,2,1,0:T(8,128)S(1)}, f32[4,4,128,128]{3,2,1,0:T(8,128)}, u32[]{:S(2)}) copy-start(f32[4,4,128,128]{3,2,1,0:T(8,128)} %ham.1) | copy-start | bytes 3145732
  1.9 0.7 %copy-start.1 = (s32[4,4]{1,0:T(4,128)S(1)}, s32[4,4]{1,0:T(4,128)}, u32[]{:S(2)}) copy-start(s32[4,4]{1,0:T(4,128)} %columns.1) | copy-start | bytes 196

commit v3 on v2

--- a/solution.py
+++ b/solution.py
@@ -65,6 +65,9 @@
     def to_behind(u):
         return copy(ham.at[own(u), pl.ds(pair * s, pair)], mine(u + 8), send.at[8 + u - 6], recv.at[u + 8, s], behind)
 
+    def last_to_behind():
+        return copy(ham.at[own(7)], ext.at[15], send.at[9], recv.at[15, 0], behind)
+
     def mine_to_peer(u):
         return copy(mine(u), mine(u), send.at[10 + u - 10], recv.at[u, s], peer)
 
@@ -148,8 +151,10 @@
         if u < 12:
             mine_to_mate(u).start()
             to_outer(17 - u).start()
-        elif u < 14:
-            to_behind(u - 6).start()
+        elif u == 12:
+            to_behind(6).start()
+        elif u == 13:
+            last_to_behind().start()
 
     def got_rest(u):
         theirs_from_peer(u).wait_recv()
@@ -207,14 +212,16 @@
 
     events = {
         0: lambda: (got(10),),
-        2: lambda: (got(11), got_rest(10)),
-        3: lambda: (from_mate(1),),
-        4: lambda: (got(12), got_rest(11)),
-        5: lambda: (from_mate(0),),
-        6: lambda: (got(13), got_rest(12)),
-        8: lambda: (got(14), got_rest(13)),
-        10: lambda: (got(15), got_rest(14)),
-        12: lambda: (got_rest(15),),
+        1: lambda: (got(11),),
+        2: lambda: (got_rest(10),),
+        3: lambda: (got(12), from_mate(1)),
+        4: lambda: (got_rest(11),),
+        5: lambda: (from_mate(0), got(13)),
+        6: lambda: (got_rest(12),),
+        7: lambda: (got(14),),
+        8: lambda: (got_rest(13),),
+        10: lambda: (got_rest(14),),
+        12: lambda: (last_to_behind().wait_recv(), begin(15)),
     }
 
     def body(turn, carry):
@@ -228,9 +235,9 @@
     for u in (9, 8, 7, 6):
         to_outer(u).wait_send()
         to_mate(u).wait_send()
-    for u in (6, 7):
-        to_behind(u).wait_send()
-    for u in range(10, 16):
+    to_behind(6).wait_send()
+    last_to_behind().wait_send()
+    for u in range(10, 15):
         mine_to_peer(u).wait_send()
         if u < 12:
             mine_to_mate(u).wait_send()
@@ -246,7 +253,7 @@
         functools.partial(kernel, devices),
         out_shape=jax.ShapeDtypeStruct(hamiltonian.shape, jnp.float32),
         in_specs=[
-            pl.BlockSpec(memory_space=pl.ANY),
+            pl.BlockSpec(memory_space=pltpu.HBM),
             pl.BlockSpec(memory_space=pltpu.VMEM),
             pl.BlockSpec(memory_space=pltpu.SMEM),
         ],

time: 38.5 us -> 37.1 us (0.964)
  Pallas kernels: 34.8 us -> 33.4 us
    pallas_call x1, Pallas kernels: 34.8 us -> 33.4 us  [shards(): pl.pallas_call(functools.partial(kernel, devices), out_shape=jax.ShapeDty...]
where the time goes in v3:
time: 37.1 us; the launch traced here: 36.9 us
  Pallas kernels  33.4 us (90%)
  local copies, waits for them, and re-layouts  2.87 us (8%)
  between operations  0.67 us (2%)
    pallas_call x1, Pallas kernels, shards(): pl.pallas_call(functools.partial(kernel, devices), out_shape=jax.ShapeDty...  33.4 us
    unnamed x5, local copies, waits for them, and re-layouts  2.87 us

profile of v3, /device:TPU:0, one launch (start us, length us, event | category | flops | bytes accessed | tf_op | source)
XLA Modules:
  0.0 36.9 jit_solution(18090809405210173949)
XLA Ops:
  0.7 0.0 copy-start
  0.7 1.2 %copy-done = f32[4,4,128,128]{3,2,1,0:T(8,128)S(1)} copy-done((f32[4,4,128,128]{3,2,1,0:T(8,128)S(1)}, f32[4,4,128,128]{3,2,1,0:T(8,128)}, u32[]{:S(2)}) %copy-start) | copy-done | bytes 1048600
  1.9 0.0 copy-start.1
  1.9 0.7 %copy-done.1 = s32[4,4]{1,0:T(4,128)S(1)} copy-done((s32[4,4]{1,0:T(4,128)S(1)}, s32[4,4]{1,0:T(4,128)}, u32[]{:S(2)}) %copy-start.1) | copy-done | bytes 88
  2.6 33.4 %shard_map.37 = f32[4,4,128,128]{3,2,1,0:T(8,128)S(1)} custom-call(f32[4,4,128,128]{3,2,1,0:T(8,128)S(1)} %copy-done, s32[4,4]{1,0:T(4,128)S(1)} %copy-done.1, s32[1]{0:T(128)S(6)} %copy.5.sample), custom_call_target="tpu_custom_call" | custom-call | tf_op jit(solution)/shard_map/pallas_call | solution.py:252
  35.9 1.0 %copy.6 = f32[4,4,128,128]{3,2,1,0:T(8,128)} copy(f32[4,4,128,128]{3,2,1,0:T(8,128)S(1)} %shard_map.37) | data formatting | bytes 2097152
Async XLA Ops:
  0.7 1.2 %copy-start = (f32[4,4,128,128]{3,2,1,0:T(8,128)S(1)}, f32[4,4,128,128]{3,2,1,0:T(8,128)}, u32[]{:S(2)}) copy-start(f32[4,4,128,128]{3,2,1,0:T(8,128)} %ham.1) | copy-start | bytes 3145732
  1.9 0.7 %copy-start.1 = (s32[4,4]{1,0:T(4,128)S(1)}, s32[4,4]{1,0:T(4,128)}, u32[]{:S(2)}) copy-start(s32[4,4]{1,0:T(4,128)} %columns.1) | copy-start | bytes 196
